TPU v7x, 128 devices: a whole 4x4x4 slice. The times are simulated.
128 devices in a mesh: seq: 8 (over x, core), grp: 16 (over z, y).
Axes of the slice: x: 4, y: 4, z: 4, core: 2. Of those that a mesh axis runs over, the one named last changes fastest.
Arguments:
- guess: float32 [2, 4096, 256], P(None, ('seq', 'grp')), may hold values from -24 to 24
- inputs: bfloat16 [2, 4096, 256], P(None, ('seq', 'grp')), may hold values from -6 to 6
- initial: float32 [2, 256], replicated, may hold values from -6 to 6
- skew_base: float32 [256, 256], replicated, may hold values from -0.09375 to 0.09375
- in_weight: bfloat16 [256, 256], replicated, may hold values from -0.375 to 0.375
- bias: float32 [256], replicated, may hold values from -3 to 3
- rate: float32 [256], replicated, may hold values from 2e-05 to 0.0001
Outputs:
- new_states: float32 [2, 4096, 256], P(None, ('seq', 'grp'))
All inputs are finite; a program needn't handle non-finite values.
Results may differ from a plain program's by a relative error of at most 0.0003.
Values sent between devices are 32-bit elements; how exact they have to be, the bound alone decides.
A program may use at most 64 MiB of HBM per device.

v0:
```python
import jax
import jax.numpy as jnp
from jax import lax
from jax.experimental import pallas as pl
from jax.experimental.pallas import tpu as pltpu
from jax.sharding import PartitionSpec as P

SEQ_GRP = ("seq", "grp")
MESH = pl.DeviceIdType.MESH
F32 = jnp.float32
BF16 = jnp.bfloat16
GAIN = 0.05

WIDTH = 256
STEPS = 32
SUB = 8
SUBS = STEPS // SUB
ROWS = WIDTH + 16
SLAB_Z = 1


def split(value):
    high = value.astype(BF16)
    return high, (value - high.astype(F32)).astype(BF16)


def dot(a, b):
    return jnp.dot(a, b, preferred_element_type=F32)


def dot3(value, high, low):
    top, rest = split(value)
    return dot(top, high) + dot(top, low) + dot(rest, high)


def first_row(rows):
    return (lax.broadcasted_iota(jnp.int32, (rows, WIDTH), 0) == 0).astype(F32)


def as_columns(row):
    turned = jnp.transpose(jnp.broadcast_to(row, (128, WIDTH)))
    return jnp.concatenate([turned, turned], axis=1)


def applied(columns, matrix, vector):
    return jnp.sum(matrix * columns, axis=0, keepdims=True) + vector


def kernel(
    guess, inputs, initial, base, weight, bias, rate, out,
    skew_hi, skew_lo, before, prev, slope, offset, chain, ymaps, ywhole, gmaps, gwhole,
    xin, xout, gin, gout, fin, fout, state, slope2, offset2, out2,
    psem, ysend, yrecv, gsend, grecv, xsem, esend, erecv, fsend, frecv,
):
    seq_at, grp_at = lax.axis_index("seq"), lax.axis_index("grp")
    x, c = seq_at // 2, seq_at % 2
    z, y = grp_at // 4, grp_at % 4
    place = x * 32 + c * 16 + z * 4 + y

    def device(x, c, z, y):
        return (x * 2 + c, z * 4 + y)

    def block(index):
        return (index // 16, index % 16)

    mine = y // 2
    yroot = c == y % 2
    slab = yroot & (c == 0) & (z == SLAB_Z)
    root_at = [2 * s + c for s in range(2)]
    slab_id = device(x, 0, SLAB_Z, 2 * mine)

    barrier = pltpu.get_barrier_semaphore()

    def greet(target):
        pl.semaphore_signal(barrier, inc=1, device_id=target, device_id_type=MESH)

    @pl.when(place > 0)
    def _():
        greet(block(place - 1))

    for s in range(2):

        @pl.when(root_at[s] != y)
        def _():
            greet(device(x, c, z, root_at[s]))

    @pl.when(yroot)
    def _():
        for k in range(1, 4):
            greet(device(x, c, z, (y + k) % 4))

    @pl.when(yroot & jnp.logical_not(slab))
    def _():
        greet(slab_id)

    @pl.when(slab)
    def _():
        for k in range(8):
            if k != SLAB_Z:
                greet(device(x, k // 4, k % 4, 2 * mine + k // 4))

    @pl.when(slab & (x > 0))
    def _():
        greet(device(x - 1, c, z, y))

    skew_t = jnp.transpose(base[...]) - base[...]
    high, low = split(skew_t)
    skew_hi[...] = high
    skew_lo[...] = low
    keep = 1.0 - rate[...]
    pre = dot(inputs[...].reshape(2 * STEPS, WIDTH), weight[...]) + bias[...]
    for s in range(2):
        prev[s, 8 : 8 + STEPS, :] = guess[s]
    eye = (
        lax.broadcasted_iota(jnp.int32, (ROWS, WIDTH), 0)
        == lax.broadcasted_iota(jnp.int32, (ROWS, WIDTH), 1)
    ).astype(F32)
    for s in range(2):
        chain[0, s] = eye

    one = jnp.int32(1)
    none = jnp.int32(0)
    sends = jnp.where(place < 127, one, none) + jnp.where(yroot, one, one + one)
    sends = sends + jnp.where(yroot, one * 3, none) + jnp.where(yroot, one, none)
    sends = sends + jnp.where(slab, one * 6, none) + jnp.where(slab & (x < 3), one, none)
    pl.semaphore_wait(barrier, sends)

    ahead = jnp.minimum(place + 1, 127)
    tail = pltpu.make_async_remote_copy(
        src_ref=guess.at[:, STEPS - 8 :, :],
        dst_ref=before,
        send_sem=psem.at[0],
        recv_sem=psem.at[1],
        device_id=block(ahead),
        device_id_type=MESH,
    )

    @pl.when(place < 127)
    def _():
        tail.start()

    @pl.when(place > 0)
    def _():
        tail.wait_recv()
        for s in range(2):
            prev[s, 7:8, :] = before[s, 7:8, :]

    @pl.when(place == 0)
    def _():
        for s in range(2):
            prev[s, 7:8, :] = initial[s : s + 1, :]

    earlier = jnp.concatenate([prev[s, 7 : 7 + STEPS, :] for s in range(2)], axis=0)
    lin = dot3(earlier, skew_hi[...], skew_lo[...])
    act = jnp.tanh(lin + pre)
    steep = 1.0 - act * act
    slope[...] = GAIN * steep
    offset[...] = GAIN * (act - steep * lin)
    for half in range(2):
        lanes = slice(half * 128, half * 128 + 128)
        slope2[half] = slope[:, lanes]
        offset2[half] = offset[:, lanes]

    top = first_row(16)

    def sub_block(sub, carry):
        for inner in range(SUB):
            src = sub if inner == 0 else sub + 1
            for s in range(2):
                at = s * STEPS + sub * SUB + inner
                held = chain[src, s]
                turned = dot3(held, skew_hi[...], skew_lo[...])
                moved = keep * held + slope[pl.ds(at, 1), :] * turned
                chain[sub + 1, s, :WIDTH] = moved[:WIDTH]
                chain[sub + 1, s, WIDTH:] = moved[WIDTH:] + top * offset[pl.ds(at, 1), :]
        return carry

    lax.fori_loop(0, SUBS, sub_block, 0)

    to_root = []
    for s in range(2):
        copy = pltpu.make_async_remote_copy(
            src_ref=chain.at[SUBS, s],
            dst_ref=ymaps.at[y],
            send_sem=ysend.at[s],
            recv_sem=yrecv.at[y],
            device_id=device(x, c, z, root_at[s]),
            device_id_type=MESH,
        )
        to_root.append(copy)

        @pl.when(root_at[s] != y)
        def _():
            copy.start()

    def arrival(maps, sems, k):
        return pltpu.make_async_remote_copy(
            src_ref=maps.at[k],
            dst_ref=maps.at[k],
            send_sem=sems.at[k],
            recv_sem=sems.at[k],
            device_id=device(x, c, z, (y + 1) % 4),
            device_id_type=MESH,
        )

    def compose(whole, maps, k):
        high, low = split(maps[k, :WIDTH, :])
        joined = dot3(whole[k - 1], high, low)
        whole[k, :WIDTH] = joined[:WIDTH]
        whole[k, WIDTH:] = joined[WIDTH:] + maps[k, WIDTH:, :]

    to_slab = pltpu.make_async_remote_copy(
        src_ref=ywhole.at[3],
        dst_ref=gmaps.at[c * 4 + z],
        send_sem=gsend,
        recv_sem=grecv.at[c * 4 + z],
        device_id=slab_id,
        device_id_type=MESH,
    )

    @pl.when(yroot)
    def _():
        ymaps[y] = chain[SUBS, mine]
        for k in range(4):

            @pl.when(y != k)
            def _():
                arrival(ymaps, yrecv, k).wait_recv()

            if k == 0:
                ywhole[0] = ymaps[0]
            else:
                compose(ywhole, ymaps, k)

    @pl.when(yroot & jnp.logical_not(slab))
    def _():
        to_slab.start()

    onward = pltpu.make_async_remote_copy(
        src_ref=xout,
        dst_ref=xin,
        send_sem=xsem.at[0],
        recv_sem=xsem.at[1],
        device_id=device(jnp.minimum(x + 1, 3), c, z, y),
        device_id_type=MESH,
    )

    def to_yroot(k):
        return pltpu.make_async_remote_copy(
            src_ref=gout.at[k],
            dst_ref=gin,
            send_sem=esend.at[k],
            recv_sem=erecv,
            device_id=device(x, k // 4, k % 4, 2 * mine + k // 4),
            device_id_type=MESH,
        )

    @pl.when(slab)
    def _():
        gmaps[SLAB_Z] = ywhole[3]
        for k in range(8):
            if k != SLAB_Z:
                arrival(gmaps, grecv, k).wait_recv()
            if k == 0:
                gwhole[0] = gmaps[0]
            else:
                compose(gwhole, gmaps, k)

        @pl.when(x == 0)
        def _():
            xin[...] = jnp.broadcast_to(initial[pl.ds(mine, 1), :], (8, WIDTH))

        @pl.when(x > 0)
        def _():
            onward.wait_recv()

        columns = as_columns(xin[0:1, :])

        @pl.when(x < 3)
        def _():
            after = applied(columns, gwhole[7, :WIDTH, :], gwhole[7, WIDTH : WIDTH + 1, :])
            xout[...] = jnp.broadcast_to(after, (8, WIDTH))
            onward.start()

        for k in range(8):
            if k == 0:
                gout[0] = xin[...]
            else:
                entry = applied(
                    columns, gwhole[k - 1, :WIDTH, :], gwhole[k - 1, WIDTH : WIDTH + 1, :]
                )
                gout[k] = jnp.broadcast_to(entry, (8, WIDTH))
            if k != SLAB_Z:
                to_yroot(k).start()
            else:
                gin[...] = gout[k]

    def to_block(k):
        return pltpu.make_async_remote_copy(
            src_ref=fout.at[k],
            dst_ref=fin.at[mine],
            send_sem=fsend.at[k],
            recv_sem=frecv.at[mine],
            device_id=device(x, c, z, k),
            device_id_type=MESH,
        )

    @pl.when(yroot & jnp.logical_not(slab))
    def _():
        to_yroot(0).wait_recv()

    @pl.when(yroot)
    def _():
        columns = as_columns(gin[0:1, :])
        for k in range(4):
            if k == 0:
                fout[0] = gin[...]
            else:
                entry = applied(
                    columns, ywhole[k - 1, :WIDTH, :], ywhole[k - 1, WIDTH : WIDTH + 1, :]
                )
                fout[k] = jnp.broadcast_to(entry, (8, WIDTH))

            @pl.when(y != k)
            def _():
                to_block(k).start()

            @pl.when(y == k)
            def _():
                fin[mine] = fout[k]

    for s in range(2):

        @pl.when(root_at[s] != y)
        def _():
            pltpu.make_async_remote_copy(
                src_ref=fin.at[s],
                dst_ref=fin.at[s],
                send_sem=frecv.at[s],
                recv_sem=frecv.at[s],
                device_id=device(x, c, z, (y + 1) % 4),
                device_id_type=MESH,
            ).wait_recv()

    for s in range(2):
        row = fin[s, 0:1, :]
        columns = as_columns(row)
        state[s * SUBS : s * SUBS + 1, :] = row
        for sub in range(1, SUBS):
            at = s * SUBS + sub
            state[at : at + 1, :] = applied(
                columns, chain[sub, s, :WIDTH, :], chain[sub, s, WIDTH : WIDTH + 1, :]
            )
    now = state[...]
    for inner in range(SUB):
        turned = dot3(now, skew_hi[...], skew_lo[...])
        at = pl.ds(inner, 2 * SUBS, stride=SUB)
        steep = jnp.concatenate([slope2[half, at, :] for half in range(2)], axis=1)
        added = jnp.concatenate([offset2[half, at, :] for half in range(2)], axis=1)
        now = keep * now + steep * turned + added
        for half in range(2):
            out2[half, at, :] = now[:, half * 128 : half * 128 + 128]
    for half in range(2):
        out[:, half * 128 : half * 128 + 128] = out2[half]

    @pl.when(place < 127)
    def _():
        tail.wait_send()

    for s in range(2):

        @pl.when(root_at[s] != y)
        def _():
            to_root[s].wait_send()

    @pl.when(yroot & jnp.logical_not(slab))
    def _():
        to_slab.wait_send()

    @pl.when(slab & (x < 3))
    def _():
        onward.wait_send()

    @pl.when(slab)
    def _():
        for k in range(8):
            if k != SLAB_Z:
                to_yroot(k).wait_send()

    @pl.when(yroot)
    def _():
        for k in range(4):

            @pl.when(y != k)
            def _():
                to_block(k).wait_send()


def per_device(guess, inputs, initial, skew_base, in_weight, bias, rate):
    vmem = pl.BlockSpec(memory_space=pltpu.VMEM)
    dma = pltpu.SemaphoreType.DMA
    states = pl.pallas_call(
        kernel,
        out_shape=jax.ShapeDtypeStruct((2 * STEPS, WIDTH), F32),
        in_specs=[vmem] * 7,
        out_specs=vmem,
        scratch_shapes=[
            pltpu.VMEM((WIDTH, WIDTH), BF16),
            pltpu.VMEM((WIDTH, WIDTH), BF16),
            pltpu.VMEM((2, 8, WIDTH), F32),
            pltpu.VMEM((2, STEPS + 8, WIDTH), F32),
            pltpu.VMEM((2 * STEPS, WIDTH), F32),
            pltpu.VMEM((2 * STEPS, WIDTH), F32),
            pltpu.VMEM((SUBS + 1, 2, ROWS, WIDTH), F32),
            pltpu.VMEM((4, ROWS, WIDTH), F32),
            pltpu.VMEM((4, ROWS, WIDTH), F32),
            pltpu.VMEM((8, ROWS, WIDTH), F32),
            pltpu.VMEM((8, ROWS, WIDTH), F32),
            pltpu.VMEM((8, WIDTH), F32),
            pltpu.VMEM((8, WIDTH), F32),
            pltpu.VMEM((8, WIDTH), F32),
            pltpu.VMEM((8, 8, WIDTH), F32),
            pltpu.VMEM((2, 8, WIDTH), F32),
            pltpu.VMEM((4, 8, WIDTH), F32),
            pltpu.VMEM((8, WIDTH), F32),
            pltpu.VMEM((2, 2 * STEPS, 128), F32),
            pltpu.VMEM((2, 2 * STEPS, 128), F32),
            pltpu.VMEM((2, 2 * STEPS, 128), F32),
            dma((2,)),
            dma((2,)),
            dma((4,)),
            dma,
            dma((8,)),
            dma((2,)),
            dma((8,)),
            dma,
            dma((4,)),
            dma((2,)),
        ],
        compiler_params=pltpu.CompilerParams(
            collective_id=0, has_side_effects=True, vmem_limit_bytes=48 * 1024 * 1024
        ),
    )(
        guess,
        inputs,
        initial,
        skew_base,
        in_weight,
        bias.reshape(1, WIDTH),
        rate.reshape(1, WIDTH),
    )
    return states.reshape(2, STEPS, WIDTH)


def solution(mesh):
    return jax.shard_map(
        per_device,
        mesh=mesh,
        in_specs=(P(None, SEQ_GRP, None), P(None, SEQ_GRP, None), P(), P(), P(), P(), P()),
        out_specs=P(None, SEQ_GRP, None),
        check_vma=False,
    )
```

profile of v0, /device:TPU:6, one launch (start us, length us, event | category | flops | bytes accessed | tf_op | source)
XLA Modules:
  0.0 63.2 jit_solution(10637986207621427190)
XLA Ops:
  0.0 0.0 copy-start.4
  0.0 0.0 copy-start.5
  0.0 0.7 %copy-done.4 = f32[2,256]{1,0:T(2,128)S(1)} copy-done((f32[2,256]{1,0:T(2,128)S(1)}, f32[2,256]{1,0:T(2,128)}, u32[]{:S(2)}) %copy-start.4) | copy-done | bytes 2072
  0.7 0.0 copy-done.5
  0.7 0.0 copy-start
  0.7 0.9 %copy-done = f32[256,256]{1,0:T(8,128)S(1)} copy-done((f32[256,256]{1,0:T(8,128)S(1)}, f32[256,256]{1,0:T(8,128)}, u32[]{:S(2)}) %copy-start) | copy-done | bytes 262168
  1.6 0.0 copy-start.1
  1.6 0.9 %copy-done.1 = bf16[256,256]{1,0:T(8,128)(2,1)S(1)} copy-done((bf16[256,256]{1,0:T(8,128)(2,1)S(1)}, bf16[256,256]{1,0:T(8,128)(2,1)}, u32[]{:S(2)}) %copy-start.1) | copy-done | bytes 131096
  2.6 0.0 copy-start.2
  2.6 0.8 %copy-done.2 = f32[2,32,256]{2,1,0:T(8,128)S(1)} copy-done((f32[2,32,256]{2,1,0:T(8,128)S(1)}, f32[2,32,256]{2,1,0:T(8,128)}, u32[]{:S(2)}) %copy-start.2) | copy-done | bytes 65560
  3.4 0.0 copy-start.3
  3.4 0.8 %copy-done.3 = bf16[2,32,256]{2,1,0:T(8,128)(2,1)S(1)} copy-done((bf16[2,32,256]{2,1,0:T(8,128)(2,1)S(1)}, bf16[2,32,256]{2,1,0:T(8,128)(2,1)}, u32[]{:S(2)}) %copy-start.3) | copy-done | bytes 32792
  4.1 0.0 copy-start.6
  4.2 0.7 %copy-done.6 = f32[256]{0:T(256)S(1)} copy-done((f32[256]{0:T(256)S(1)}, f32[256]{0:T(256)}, u32[]{:S(2)}) %copy-start.6) | copy-done | bytes 1048
  4.8 57.8 %shard_map.73 = f32[64,256]{1,0:T(8,128)S(1)} custom-call(f32[2,32,256]{2,1,0:T(8,128)S(1)} %copy-done.2, bf16[2,32,256]{2,1,0:T(8,128)(2,1)S(1)} %copy-done.3, f32[2,256]{1,0:T(2,128)S(1)} %copy-done.4, f32[256,256]{1,0:T(8,128)S(1)} %copy-done, bf16[256,256]{1,0:T(8,128)(2,1)S(1)} %copy-done.1, f32[1,256]{1,0:T(1,128)S(1)} %bitcast.4, f32[1,256]{1,0:T(1,128)S(1)} %bitcast.5), custom_call_target="tpu_custom_call" | custom-call | tf_op jit(solution)/shard_map/pallas_call | solution.py:402
  62.6 0.6 copy.9
Async XLA Ops:
  0.0 0.7 %copy-start.4 = (f32[2,256]{1,0:T(2,128)S(1)}, f32[2,256]{1,0:T(2,128)}, u32[]{:S(2)}) copy-start(f32[2,256]{1,0:T(2,128)} %initial.1) | copy-start | bytes 6148
  0.0 0.7 %copy-start.5 = (f32[256]{0:T(256)S(1)}, f32[256]{0:T(256)}, u32[]{:S(2)}) copy-start(f32[256]{0:T(256)} %param.12) | copy-start | bytes 3076
  0.7 0.9 %copy-start = (f32[256,256]{1,0:T(8,128)S(1)}, f32[256,256]{1,0:T(8,128)}, u32[]{:S(2)}) copy-start(f32[256,256]{1,0:T(8,128)} %base.1) | copy-start | bytes 786436
  1.6 0.9 %copy-start.1 = (bf16[256,256]{1,0:T(8,128)(2,1)S(1)}, bf16[256,256]{1,0:T(8,128)(2,1)}, u32[]{:S(2)}) copy-start(bf16[256,256]{1,0:T(8,128)(2,1)} %weight.1) | copy-start | bytes 393220
  2.6 0.8 %copy-start.2 = (f32[2,32,256]{2,1,0:T(8,128)S(1)}, f32[2,32,256]{2,1,0:T(8,128)}, u32[]{:S(2)}) copy-start(f32[2,32,256]{2,1,0:T(8,128)} %guess.1) | copy-start | bytes 196612
  3.4 0.8 %copy-start.3 = (bf16[2,32,256]{2,1,0:T(8,128)(2,1)S(1)}, bf16[2,32,256]{2,1,0:T(8,128)(2,1)}, u32[]{:S(2)}) copy-start(bf16[2,32,256]{2,1,0:T(8,128)(2,1)} %inputs.1) | copy-start | bytes 98308
  4.1 0.7 %copy-start.6 = (f32[256]{0:T(256)S(1)}, f32[256]{0:T(256)}, u32[]{:S(2)}) copy-start(f32[256]{0:T(256)} %param.13) | copy-start | bytes 3076
where the time goes:
time: 63.5 us; the launch traced here: 63.2 us
  Pallas kernels  57.8 us (91%)
  local copies, waits for them, and re-layouts  5.45 us (9%)
    pallas_call x1, Pallas kernels, per_device(): pl.pallas_call(kernel, out_shape=jax.ShapeDtypeStruct((2 * STEPS, WIDTH),...  57.8 us
    unnamed x15, local copies, waits for them, and re-layouts  5.45 us

commit v1 on v0

v1 whole, which is shorter than its diff:
```python
import jax
import jax.numpy as jnp
from jax import lax
from jax.experimental import pallas as pl
from jax.experimental.pallas import tpu as pltpu
from jax.sharding import PartitionSpec as P

SEQ_GRP = ("seq", "grp")
MESH = pl.DeviceIdType.MESH
F32 = jnp.float32
BF16 = jnp.bfloat16
GAIN = 0.05

WIDTH = 256
STEPS = 32
SUB = 8
SUBS = STEPS // SUB
ROWS = WIDTH + 16
ZROOT = 1


def split(value):
    high = value.astype(BF16)
    return high, (value - high.astype(F32)).astype(BF16)


def dot(a, b):
    return jnp.dot(a, b, preferred_element_type=F32)


def dot3(value, high, low):
    top, rest = split(value)
    return dot(top, high) + dot(top, low) + dot(rest, high)


def compose(target, left, right):
    high, low = split(right[:WIDTH, :])
    joined = dot3(left[...], high, low)
    target[:WIDTH, :] = joined[:WIDTH]
    target[WIDTH:, :] = joined[WIDTH:] + right[WIDTH:, :]


def as_columns(row):
    turned = jnp.transpose(jnp.broadcast_to(row, (128, WIDTH)))
    return jnp.concatenate([turned, turned], axis=1)


def applied(columns, whole):
    moved = jnp.sum(whole[:WIDTH, :] * columns, axis=0, keepdims=True)
    return moved + whole[WIDTH : WIDTH + 1, :]


def tile(row):
    return jnp.broadcast_to(row, (8, WIDTH))


def kernel(
    guess_in, inputs_in, initial_in, base_in, weight_in, bias_in, rate_in, out,
    guess, inputs, initial, base, weight, bias, rate,
    skew, skew_hi, skew_lo, diag, before, prev, pre, slope, offset, slope2, offset2, out2,
    part, start, first, second, third, own,
    ymaps, ywhole, zmaps, zwhole, half, whole,
    xin, cin, ein, xout, cout, zout, zin, fout, fin, state,
    isem, psem, ysend, yrecv, zsend, zrecv, hsem, csem, xsend, xrecv, esend, erecv, fsend, frecv,
):
    seq_at, grp_at = lax.axis_index("seq"), lax.axis_index("grp")
    x, c = seq_at // 2, seq_at % 2
    z, y = grp_at // 4, grp_at % 4
    place = x * 32 + c * 16 + z * 4 + y

    def device(x, c, z, y):
        return (x * 2 + c, z * 4 + y)

    def block(index):
        return (index // 16, index % 16)

    mine = y // 2
    yroot = c == y % 2
    zroot = yroot & (z == ZROOT)
    below = yroot & (z != ZROOT)
    zroot0 = zroot & (c == 0)
    zroot1 = zroot & (c == 1)
    root_at = [2 * s + c for s in range(2)]

    def zroot_id(x, c):
        return device(x, c, ZROOT, 2 * mine + c)

    fetches = [
        pltpu.make_async_copy(source, target, isem.at[index])
        for index, (source, target) in enumerate(
            (
                (guess_in, guess),
                (inputs_in, inputs),
                (initial_in, initial),
                (base_in, base),
                (weight_in, weight),
                (bias_in, bias),
                (rate_in, rate),
            )
        )
    ]
    for index in (3, 6, 0, 1, 4, 5, 2):
        fetches[index].start()

    barrier = pltpu.get_barrier_semaphore()

    def greet(target):
        pl.semaphore_signal(barrier, inc=1, device_id=target, device_id_type=MESH)

    @pl.when(place > 0)
    def _():
        greet(block(place - 1))

    for s in range(2):

        @pl.when(root_at[s] != y)
        def _():
            greet(device(x, c, z, root_at[s]))

    @pl.when(yroot)
    def _():
        for k in range(1, 4):
            greet(device(x, c, z, (y + k) % 4))

    @pl.when(below)
    def _():
        greet(device(x, c, ZROOT, y))

    @pl.when(zroot)
    def _():
        for k in range(4):
            if k != ZROOT:
                greet(device(x, c, k, y))

    @pl.when(zroot1)
    def _():
        greet(zroot_id(x, 0))

    @pl.when(zroot & (x > 0))
    def _():
        greet(zroot_id(x - 1, 1))

    fetches[3].wait()
    skew_t = jnp.transpose(base[...]) - base[...]
    skew[...] = skew_t
    high, low = split(skew_t)
    skew_hi[...] = high
    skew_lo[...] = low
    fetches[6].wait()
    keep = 1.0 - rate[...]
    square = (WIDTH, WIDTH)
    eye = lax.broadcasted_iota(jnp.int32, square, 0) == lax.broadcasted_iota(jnp.int32, square, 1)
    diag[...] = jnp.where(eye, jnp.broadcast_to(keep, square), 0.0)
    top = (lax.broadcasted_iota(jnp.int32, (16, WIDTH), 0) == 0).astype(F32)

    fetches[0].wait()
    for s in range(2):
        prev[s, 0:8, :] = jnp.zeros((8, WIDTH), F32)
        prev[s, 8 : 8 + STEPS, :] = guess[s]
    for index in (1, 4, 5, 2):
        fetches[index].wait()
    pre[...] = dot(inputs[...].reshape(2 * STEPS, WIDTH), weight[...]) + bias[...]

    def slopes(earlier, before_tanh):
        lin = dot3(earlier, skew_hi[...], skew_lo[...])
        act = jnp.tanh(lin + before_tanh)
        steep = 1.0 - act * act
        return GAIN * steep, GAIN * (act - steep * lin)

    def keep_slopes(rows, steep, added):
        slope[rows, :] = steep
        offset[rows, :] = added
        for part_at in range(2):
            lanes = slice(part_at * 128, part_at * 128 + 128)
            slope2[part_at, rows, :] = steep[:, lanes]
            offset2[part_at, rows, :] = added[:, lanes]

    earlier = jnp.concatenate([prev[s, 7 : 7 + STEPS, :] for s in range(2)], axis=0)
    keep_slopes(slice(0, 2 * STEPS), *slopes(earlier, pre[...]))

    one, none = jnp.int32(1), jnp.int32(0)
    sends = jnp.where(place < 127, one, none) + jnp.where(yroot, 4 * one, 2 * one)
    sends = sends + jnp.where(below, one, none) + jnp.where(zroot, 3 * one, none)
    sends = sends + jnp.where(zroot0, one, none) + jnp.where(zroot1 & (x < 3), 2 * one, none)
    pl.semaphore_wait(barrier, sends)

    tail = pltpu.make_async_remote_copy(
        src_ref=guess.at[:, STEPS - 8 :, :],
        dst_ref=before,
        send_sem=psem.at[0],
        recv_sem=psem.at[1],
        device_id=block(jnp.minimum(place + 1, 127)),
        device_id_type=MESH,
    )

    @pl.when(place < 127)
    def _():
        tail.start()

    def of_step(target, at):
        target[:WIDTH, :] = diag[...] + skew[...] * slope[at : at + 1, :]
        target[WIDTH:, :] = top * offset[at : at + 1, :]

    def chains(s):
        for sub in range(SUBS):
            of_step(part.at[s, sub], s * STEPS + max(sub * SUB, 1))
        for inner in range(1, SUB):
            for sub in range(SUBS):
                at = max(sub * SUB, 1) + inner
                if at == SUB * (sub + 1):
                    continue
                at = at + s * STEPS
                held = part[s, sub]
                turned = dot3(held, skew_hi[...], skew_lo[...])
                moved = keep * held + slope[at : at + 1, :] * turned
                part[s, sub, :WIDTH, :] = moved[:WIDTH]
                part[s, sub, WIDTH:, :] = moved[WIDTH:] + top * offset[at : at + 1, :]

    def to_root(s):
        return pltpu.make_async_remote_copy(
            src_ref=own.at[s],
            dst_ref=ymaps.at[y],
            send_sem=ysend.at[s],
            recv_sem=yrecv.at[y],
            device_id=device(x, c, z, root_at[s]),
            device_id_type=MESH,
        )

    def landed(buffer, sem):
        return pltpu.make_async_remote_copy(
            src_ref=buffer,
            dst_ref=buffer,
            send_sem=sem,
            recv_sem=sem,
            device_id=device(x, c, z, (y + 1) % 4),
            device_id_type=MESH,
        )

    for s in range(2):
        chains(s)
        if s == 0:

            @pl.when(place > 0)
            def _():
                tail.wait_recv()
                for t in range(2):
                    prev[t, 7:8, :] = before[t, 7:8, :]

            @pl.when(place == 0)
            def _():
                for t in range(2):
                    prev[t, 7:8, :] = initial[t : t + 1, :]

            earlier = jnp.concatenate([prev[t, 7:15, :] for t in range(2)], axis=0)
            wanted = jnp.concatenate([pre[t * STEPS : t * STEPS + 8, :] for t in range(2)], axis=0)
            steep, added = slopes(earlier, wanted)
            for t in range(2):
                rows = slice(t * 8, t * 8 + 8)
                keep_slopes(slice(t * STEPS, t * STEPS + 8), steep[rows], added[rows])
        of_step(start, s * STEPS)
        compose(third, part.at[s, 2], part.at[s, 3])
        compose(first.at[s], start, part.at[s, 0])
        compose(second.at[s], first.at[s], part.at[s, 1])
        compose(own.at[s], second.at[s], third)

        @pl.when(root_at[s] != y)
        def _():
            to_root(s).start()

    to_zroot = pltpu.make_async_remote_copy(
        src_ref=ywhole.at[3],
        dst_ref=zmaps.at[z],
        send_sem=zsend,
        recv_sem=zrecv.at[z],
        device_id=device(x, c, ZROOT, y),
        device_id_type=MESH,
    )

    @pl.when(yroot)
    def _():
        ymaps[y] = own[mine]
        for k in range(4):

            @pl.when(y != k)
            def _():
                landed(ymaps.at[k], yrecv.at[k]).wait_recv()

            if k > 0:
                compose(ywhole.at[k], ymaps.at[0] if k == 1 else ywhole.at[k - 1], ymaps.at[k])

    @pl.when(below)
    def _():
        to_zroot.start()

    across = pltpu.make_async_remote_copy(
        src_ref=zwhole.at[3],
        dst_ref=half,
        send_sem=hsem.at[0],
        recv_sem=hsem.at[1],
        device_id=zroot_id(x, 1),
        device_id_type=MESH,
    )
    across0 = pltpu.make_async_remote_copy(
        src_ref=cout,
        dst_ref=cin,
        send_sem=csem.at[0],
        recv_sem=csem.at[1],
        device_id=zroot_id(x, 1),
        device_id_type=MESH,
    )

    def onward(core):
        return pltpu.make_async_remote_copy(
            src_ref=xout,
            dst_ref=xin,
            send_sem=xsend.at[core],
            recv_sem=xrecv,
            device_id=zroot_id(jnp.minimum(x + 1, 3), core),
            device_id_type=MESH,
        )

    def to_yroot(k):
        return pltpu.make_async_remote_copy(
            src_ref=zout.at[k],
            dst_ref=zin,
            send_sem=esend.at[k],
            recv_sem=erecv,
            device_id=device(x, c, k, y),
            device_id_type=MESH,
        )

    def zprefix(k):
        return zmaps.at[0] if k == 0 else zwhole.at[k]

    @pl.when(zroot)
    def _():
        for k in range(4):
            if k != ZROOT:
                landed(zmaps.at[k], zrecv.at[k]).wait_recv()
            if k > 0:
                compose(zwhole.at[k], zprefix(k - 1), ywhole.at[3] if k == ZROOT else zmaps.at[k])

        @pl.when((c == 0) & (x == 0))
        def _():
            given = initial[pl.ds(mine, 1), :]
            ein[...] = tile(given)
            cout[...] = tile(applied(as_columns(given), zwhole.at[3]))
            across0.start()

        @pl.when((c == 0) & (x > 0))
        def _():
            across.start()
            landed(xin, xrecv).wait_recv()
            ein[...] = xin[...]

        @pl.when((c == 1) & (x == 0))
        def _():
            across0.wait_recv()
            ein[...] = cin[...]
            xout[...] = tile(applied(as_columns(cin[0:1, :]), zwhole.at[3]))
            for core in (1, 0):
                onward(core).start()

        @pl.when((c == 1) & (x > 0))
        def _():
            across.wait_recv()
            compose(whole, half, zwhole.at[3])
            landed(xin, xrecv).wait_recv()
            columns = as_columns(xin[0:1, :])

            @pl.when(x < 3)
            def _():
                xout[...] = tile(applied(columns, whole))
                for core in (1, 0):
                    onward(core).start()

            ein[...] = tile(applied(columns, half))

        columns = as_columns(ein[0:1, :])
        for k in range(4):
            zout[k] = ein[...] if k == 0 else tile(applied(columns, zprefix(k - 1)))
            if k == ZROOT:
                zin[...] = zout[k]
            else:
                to_yroot(k).start()

    def to_block(k):
        return pltpu.make_async_remote_copy(
            src_ref=fout.at[k],
            dst_ref=fin.at[mine],
            send_sem=fsend.at[k],
            recv_sem=frecv.at[mine],
            device_id=device(x, c, z, k),
            device_id_type=MESH,
        )

    @pl.when(below)
    def _():
        landed(zin, erecv).wait_recv()

    @pl.when(yroot)
    def _():
        columns = as_columns(zin[0:1, :])
        for k in range(4):
            if k == 0:
                fout[0] = zin[...]
            else:
                fout[k] = tile(applied(columns, ymaps.at[0] if k == 1 else ywhole.at[k - 1]))

            @pl.when(y != k)
            def _():
                to_block(k).start()

            @pl.when(y == k)
            def _():
                fin[mine] = fout[k]

    for s in range(2):

        @pl.when(root_at[s] != y)
        def _():
            landed(fin.at[s], frecv.at[s]).wait_recv()

    for s in range(2):
        entry = fin[s, 0:1, :]
        columns = as_columns(entry)
        middle = applied(columns, second.at[s])
        at = s * SUBS
        state[at : at + 1, :] = entry
        state[at + 1 : at + 2, :] = applied(columns, first.at[s])
        state[at + 2 : at + 3, :] = middle
        state[at + 3 : at + 4, :] = applied(as_columns(middle), part.at[s, 2])
    now = state[...]
    for inner in range(SUB):
        turned = dot3(now, skew_hi[...], skew_lo[...])
        at = pl.ds(inner, 2 * SUBS, stride=SUB)
        steep = jnp.concatenate([slope2[lanes, at, :] for lanes in range(2)], axis=1)
        added = jnp.concatenate([offset2[lanes, at, :] for lanes in range(2)], axis=1)
        now = keep * now + steep * turned + added
        for lanes in range(2):
            out2[lanes, at, :] = now[:, lanes * 128 : lanes * 128 + 128]
    for lanes in range(2):
        out[:, lanes * 128 : lanes * 128 + 128] = out2[lanes]

    @pl.when(place < 127)
    def _():
        tail.wait_send()

    for s in range(2):

        @pl.when(root_at[s] != y)
        def _():
            to_root(s).wait_send()

    @pl.when(below)
    def _():
        to_zroot.wait_send()

    @pl.when(zroot0 & (x == 0))
    def _():
        across0.wait_send()

    @pl.when(zroot0 & (x > 0))
    def _():
        across.wait_send()

    @pl.when(zroot1 & (x < 3))
    def _():
        for core in (1, 0):
            onward(core).wait_send()

    @pl.when(zroot)
    def _():
        for k in range(4):
            if k != ZROOT:
                to_yroot(k).wait_send()

    @pl.when(yroot)
    def _():
        for k in range(4):

            @pl.when(y != k)
            def _():
                to_block(k).wait_send()


def per_device(guess, inputs, initial, skew_base, in_weight, bias, rate):
    dma = pltpu.SemaphoreType.DMA

    def f32(*shape):
        return pltpu.VMEM(shape, F32)

    maps = (ROWS, WIDTH)
    states = pl.pallas_call(
        kernel,
        out_shape=jax.ShapeDtypeStruct((2 * STEPS, WIDTH), F32),
        in_specs=[pl.BlockSpec(memory_space=pl.ANY)] * 7,
        out_specs=pl.BlockSpec(memory_space=pltpu.VMEM),
        scratch_shapes=[
            f32(2, STEPS, WIDTH),
            pltpu.VMEM((2, STEPS, WIDTH), BF16),
            f32(2, WIDTH),
            f32(WIDTH, WIDTH),
            pltpu.VMEM((WIDTH, WIDTH), BF16),
            f32(1, WIDTH),
            f32(1, WIDTH),
            f32(WIDTH, WIDTH),
            pltpu.VMEM((WIDTH, WIDTH), BF16),
            pltpu.VMEM((WIDTH, WIDTH), BF16),
            f32(WIDTH, WIDTH),
            f32(2, 8, WIDTH),
            f32(2, STEPS + 8, WIDTH),
            f32(2 * STEPS, WIDTH),
            f32(2 * STEPS, WIDTH),
            f32(2 * STEPS, WIDTH),
            f32(2, 2 * STEPS, 128),
            f32(2, 2 * STEPS, 128),
            f32(2, 2 * STEPS, 128),
            f32(2, SUBS, *maps),
            f32(*maps),
            f32(2, *maps),
            f32(2, *maps),
            f32(*maps),
            f32(2, *maps),
            f32(4, *maps),
            f32(4, *maps),
            f32(4, *maps),
            f32(4, *maps),
            f32(*maps),
            f32(*maps),
            f32(8, WIDTH),
            f32(8, WIDTH),
            f32(8, WIDTH),
            f32(8, WIDTH),
            f32(8, WIDTH),
            f32(4, 8, WIDTH),
            f32(8, WIDTH),
            f32(4, 8, WIDTH),
            f32(2, 8, WIDTH),
            f32(8, WIDTH),
            dma((7,)),
            dma((2,)),
            dma((2,)),
            dma((4,)),
            dma,
            dma((4,)),
            dma((2,)),
            dma((2,)),
            dma((2,)),
            dma,
            dma((4,)),
            dma,
            dma((4,)),
            dma((2,)),
        ],
        compiler_params=pltpu.CompilerParams(
            collective_id=0, has_side_effects=True, vmem_limit_bytes=60 * 1024 * 1024
        ),
    )(
        guess,
        inputs,
        initial,
        skew_base,
        in_weight,
        bias.reshape(1, WIDTH),
        rate.reshape(1, WIDTH),
    )
    return states.reshape(2, STEPS, WIDTH)


def solution(mesh):
    return jax.shard_map(
        per_device,
        mesh=mesh,
        in_specs=(P(None, SEQ_GRP, None), P(None, SEQ_GRP, None), P(), P(), P(), P(), P()),
        out_specs=P(None, SEQ_GRP, None),
        check_vma=False,
    )
```

time: 63.5 us -> 52.3 us (0.82)
  Pallas kernels: 57.8 us -> 50.6 us
  local copies, waits for them, and re-layouts: 5.45 us -> 1.47 us
    pallas_call x1, Pallas kernels: 57.8 us -> 50.6 us  [per_device(): pl.pallas_call(kernel, out_shape=jax.ShapeDtypeStruct((2 * STEPS, WIDTH),...]
    unnamed x15 -> x1, local copies, waits for them, and re-layouts: 5.45 us -> 1.47 us
where the time goes in v1:
time: 52.3 us; the launch traced here: 52.1 us
  Pallas kernels  50.6 us (97%)
  local copies, waits for them, and re-layouts  1.47 us (3%)
    pallas_call x1, Pallas kernels, per_device(): pl.pallas_call(kernel, out_shape=jax.ShapeDtypeStruct((2 * STEPS, WIDTH),...  50.6 us
    unnamed x1, local copies, waits for them, and re-layouts  1.47 us

profile of v1, /device:TPU:6, one launch (start us, length us, event | category | flops | bytes accessed | tf_op | source)
XLA Modules:
  0.0 52.1 jit_solution(13593184012957820588)
XLA Ops:
  0.0 50.6 %shard_map.73 = f32[64,256]{1,0:T(8,128)} custom-call(f32[2,32,256]{2,1,0:T(8,128)} %guess_in.1, bf16[2,32,256]{2,1,0:T(8,128)(2,1)} %inputs_in.1, f32[2,256]{1,0:T(2,128)} %initial_in.1, f32[256,256]{1,0:T(8,128)} %base_in.1, bf16[256,256]{1,0:T(8,128)(2,1)} %weight_in.1, f32[1,256]{1,0:T(1,128)} %bitcast.4, f32[1,256]{1,0:T(1,128)} %bitcast.5), custom_call_target="tpu_custom_call" | custom-call | tf_op jit(solution)/shard_map/pallas_call | solution.py:494
  50.7 1.5 %copy.9 = f32[2,32,256]{2,1,0:T(8,128)} copy(f32[2,32,256]{2,1,0:T(8,128)} %bitcast.3) | data formatting | bytes 131072

commit v2 on v1

--- a/solution.py
+++ b/solution.py
@@ -60,7 +60,7 @@
     skew, skew_hi, skew_lo, diag, before, prev, pre, slope, offset, slope2, offset2, out2,
     part, start, first, second, third, own,
     ymaps, ywhole, zmaps, zwhole, half, whole,
-    xin, cin, ein, xout, cout, zout, zin, fout, fin, state,
+    pmaps, xin, cin, ein, xout, cout, zout, fin, entries, state,
     isem, psem, ysend, yrecv, zsend, zrecv, hsem, csem, xsend, xrecv, esend, erecv, fsend, frecv,
 ):
     seq_at, grp_at = lax.axis_index("seq"), lax.axis_index("grp")
@@ -122,15 +122,17 @@
         for k in range(1, 4):
             greet(device(x, c, z, (y + k) % 4))
 
-    @pl.when(below)
-    def _():
-        greet(device(x, c, ZROOT, y))
-
     @pl.when(zroot)
     def _():
         for k in range(4):
             if k != ZROOT:
                 greet(device(x, c, k, y))
+
+    for s in range(2):
+
+        @pl.when(jnp.logical_not(zroot & (mine == s)))
+        def _():
+            greet(device(x, c, ZROOT, root_at[s]))
 
     @pl.when(zroot1)
     def _():
@@ -178,33 +180,16 @@
     earlier = jnp.concatenate([prev[s, 7 : 7 + STEPS, :] for s in range(2)], axis=0)
     keep_slopes(slice(0, 2 * STEPS), *slopes(earlier, pre[...]))
 
-    one, none = jnp.int32(1), jnp.int32(0)
-    sends = jnp.where(place < 127, one, none) + jnp.where(yroot, 4 * one, 2 * one)
-    sends = sends + jnp.where(below, one, none) + jnp.where(zroot, 3 * one, none)
-    sends = sends + jnp.where(zroot0, one, none) + jnp.where(zroot1 & (x < 3), 2 * one, none)
-    pl.semaphore_wait(barrier, sends)
-
-    tail = pltpu.make_async_remote_copy(
-        src_ref=guess.at[:, STEPS - 8 :, :],
-        dst_ref=before,
-        send_sem=psem.at[0],
-        recv_sem=psem.at[1],
-        device_id=block(jnp.minimum(place + 1, 127)),
-        device_id_type=MESH,
-    )
-
-    @pl.when(place < 127)
-    def _():
-        tail.start()
-
     def of_step(target, at):
         target[:WIDTH, :] = diag[...] + skew[...] * slope[at : at + 1, :]
         target[WIDTH:, :] = top * offset[at : at + 1, :]
 
-    def chains(s):
-        for sub in range(SUBS):
-            of_step(part.at[s, sub], s * STEPS + max(sub * SUB, 1))
-        for inner in range(1, SUB):
+    def chains(s, begin, end):
+        for inner in range(begin, end):
+            if inner == 0:
+                for sub in range(SUBS):
+                    of_step(part.at[s, sub], s * STEPS + max(sub * SUB, 1))
+                continue
             for sub in range(SUBS):
                 at = max(sub * SUB, 1) + inner
                 if at == SUB * (sub + 1):
@@ -216,6 +201,15 @@
                 part[s, sub, :WIDTH, :] = moved[:WIDTH]
                 part[s, sub, WIDTH:, :] = moved[WIDTH:] + top * offset[at : at + 1, :]
 
+    tail = pltpu.make_async_remote_copy(
+        src_ref=guess.at[:, STEPS - 8 :, :],
+        dst_ref=before,
+        send_sem=psem.at[0],
+        recv_sem=psem.at[1],
+        device_id=block(jnp.minimum(place + 1, 127)),
+        device_id_type=MESH,
+    )
+
     def to_root(s):
         return pltpu.make_async_remote_copy(
             src_ref=own.at[s],
@@ -236,27 +230,42 @@
             device_id_type=MESH,
         )
 
-    for s in range(2):
-        chains(s)
-        if s == 0:
-
-            @pl.when(place > 0)
-            def _():
-                tail.wait_recv()
-                for t in range(2):
-                    prev[t, 7:8, :] = before[t, 7:8, :]
-
-            @pl.when(place == 0)
-            def _():
-                for t in range(2):
-                    prev[t, 7:8, :] = initial[t : t + 1, :]
-
-            earlier = jnp.concatenate([prev[t, 7:15, :] for t in range(2)], axis=0)
-            wanted = jnp.concatenate([pre[t * STEPS : t * STEPS + 8, :] for t in range(2)], axis=0)
-            steep, added = slopes(earlier, wanted)
-            for t in range(2):
-                rows = slice(t * 8, t * 8 + 8)
-                keep_slopes(slice(t * STEPS, t * STEPS + 8), steep[rows], added[rows])
+    chains(0, 0, SUB)
+
+    one, none = jnp.int32(1), jnp.int32(0)
+    sends = jnp.where(place < 127, one, none) + jnp.where(yroot, 4 * one, 2 * one)
+    sends = sends + jnp.where(below, one, none) + jnp.where(zroot, 15 * one, none)
+    sends = sends + jnp.where(zroot0, one, none) + jnp.where(zroot1 & (x < 3), 2 * one, none)
+    pl.semaphore_wait(barrier, sends)
+
+
+    @pl.when(place < 127)
+    def _():
+        tail.start()
+
+    chains(1, 0, SUB // 2)
+
+    @pl.when(place > 0)
+    def _():
+        tail.wait_recv()
+        for t in range(2):
+            prev[t, 7:8, :] = before[t, 7:8, :]
+
+    @pl.when(place == 0)
+    def _():
+        for t in range(2):
+            prev[t, 7:8, :] = initial[t : t + 1, :]
+
+    earlier = jnp.concatenate([prev[t, 7:15, :] for t in range(2)], axis=0)
+    wanted = jnp.concatenate([pre[t * STEPS : t * STEPS + 8, :] for t in range(2)], axis=0)
+    steep, added = slopes(earlier, wanted)
+    for t in range(2):
+        rows = slice(t * 8, t * 8 + 8)
+        keep_slopes(slice(t * STEPS, t * STEPS + 8), steep[rows], added[rows])
+
+    for s in range(2):
+        if s == 1:
+            chains(1, SUB // 2, SUB)
         of_step(start, s * STEPS)
         compose(third, part.at[s, 2], part.at[s, 3])
         compose(first.at[s], start, part.at[s, 0])
@@ -291,6 +300,24 @@
     @pl.when(below)
     def _():
         to_zroot.start()
+
+    def prefix_out(k):
+        return pltpu.make_async_remote_copy(
+            src_ref=ymaps.at[0] if k == 1 else ywhole.at[k - 1],
+            dst_ref=pmaps.at[mine],
+            send_sem=fsend.at[k],
+            recv_sem=frecv.at[mine],
+            device_id=device(x, c, z, k),
+            device_id_type=MESH,
+        )
+
+    @pl.when(yroot)
+    def _():
+        for k in range(1, 4):
+
+            @pl.when(y != k)
+            def _():
+                prefix_out(k).start()
 
     across = pltpu.make_async_remote_copy(
         src_ref=zwhole.at[3],
@@ -319,13 +346,13 @@
             device_id_type=MESH,
         )
 
-    def to_yroot(k):
+    def entry_out(k, at):
         return pltpu.make_async_remote_copy(
             src_ref=zout.at[k],
-            dst_ref=zin,
-            send_sem=esend.at[k],
-            recv_sem=erecv,
-            device_id=device(x, c, k, y),
+            dst_ref=fin.at[mine],
+            send_sem=esend.at[k * 4 + at],
+            recv_sem=erecv.at[mine],
+            device_id=device(x, c, k, at),
             device_id_type=MESH,
         )
 
@@ -379,50 +406,48 @@
         columns = as_columns(ein[0:1, :])
         for k in range(4):
             zout[k] = ein[...] if k == 0 else tile(applied(columns, zprefix(k - 1)))
-            if k == ZROOT:
-                zin[...] = zout[k]
-            else:
-                to_yroot(k).start()
-
-    def to_block(k):
-        return pltpu.make_async_remote_copy(
-            src_ref=fout.at[k],
-            dst_ref=fin.at[mine],
-            send_sem=fsend.at[k],
-            recv_sem=frecv.at[mine],
-            device_id=device(x, c, z, k),
-            device_id_type=MESH,
-        )
-
-    @pl.when(below)
-    def _():
-        landed(zin, erecv).wait_recv()
-
-    @pl.when(yroot)
-    def _():
-        columns = as_columns(zin[0:1, :])
-        for k in range(4):
-            if k == 0:
-                fout[0] = zin[...]
-            else:
-                fout[k] = tile(applied(columns, ymaps.at[0] if k == 1 else ywhole.at[k - 1]))
-
-            @pl.when(y != k)
-            def _():
-                to_block(k).start()
-
-            @pl.when(y == k)
-            def _():
-                fin[mine] = fout[k]
-
-    for s in range(2):
-
-        @pl.when(root_at[s] != y)
-        def _():
-            landed(fin.at[s], frecv.at[s]).wait_recv()
-
-    for s in range(2):
-        entry = fin[s, 0:1, :]
+            for at in range(4):
+                if k != ZROOT:
+                    entry_out(k, at).start()
+                else:
+
+                    @pl.when(y != at)
+                    def _():
+                        entry_out(k, at).start()
+
+        fin[mine] = zout[ZROOT]
+
+    for s in range(2):
+
+        @pl.when((y > 0) & (root_at[s] != y))
+        def _():
+            landed(pmaps.at[s], frecv.at[s]).wait_recv()
+
+    @pl.when(yroot & (y == 1))
+    def _():
+        pmaps[mine] = ymaps[0]
+
+    for k in range(2, 4):
+
+        @pl.when(yroot & (y == k))
+        def _():
+            pmaps[mine] = ywhole[k - 1]
+
+    for s in range(2):
+
+        @pl.when(jnp.logical_not(zroot & (mine == s)))
+        def _():
+            landed(fin.at[s], erecv.at[s]).wait_recv()
+
+        given = fin[s, 0:1, :]
+        entries[s] = fin[s]
+
+        @pl.when(y > 0)
+        def _():
+            entries[s] = tile(applied(as_columns(given), pmaps.at[s]))
+
+    for s in range(2):
+        entry = entries[s, 0:1, :]
         columns = as_columns(entry)
         middle = applied(columns, second.at[s])
         at = s * SUBS
@@ -472,16 +497,22 @@
     @pl.when(zroot)
     def _():
         for k in range(4):
-            if k != ZROOT:
-                to_yroot(k).wait_send()
+            for at in range(4):
+                if k != ZROOT:
+                    entry_out(k, at).wait_send()
+                else:
+
+                    @pl.when(y != at)
+                    def _():
+                        entry_out(k, at).wait_send()
 
     @pl.when(yroot)
     def _():
-        for k in range(4):
+        for k in range(1, 4):
 
             @pl.when(y != k)
             def _():
-                to_block(k).wait_send()
+                prefix_out(k).wait_send()
 
 
 def per_device(guess, inputs, initial, skew_base, in_weight, bias, rate):
@@ -494,7 +525,7 @@
     states = pl.pallas_call(
         kernel,
         out_shape=jax.ShapeDtypeStruct((2 * STEPS, WIDTH), F32),
-        in_specs=[pl.BlockSpec(memory_space=pl.ANY)] * 7,
+        in_specs=[pl.BlockSpec(memory_space=pltpu.HBM)] * 7,
         out_specs=pl.BlockSpec(memory_space=pltpu.VMEM),
         scratch_shapes=[
             f32(2, STEPS, WIDTH),
@@ -528,14 +559,14 @@
             f32(4, *maps),
             f32(*maps),
             f32(*maps),
+            f32(2, *maps),
             f32(8, WIDTH),
             f32(8, WIDTH),
             f32(8, WIDTH),
             f32(8, WIDTH),
             f32(8, WIDTH),
             f32(4, 8, WIDTH),
-            f32(8, WIDTH),
-            f32(4, 8, WIDTH),
+            f32(2, 8, WIDTH),
             f32(2, 8, WIDTH),
             f32(8, WIDTH),
             dma((7,)),
@@ -548,8 +579,8 @@
             dma((2,)),
             dma((2,)),
             dma,
-            dma((4,)),
-            dma,
+            dma((16,)),
+            dma((2,)),
             dma((4,)),
             dma((2,)),
         ],

time: 52.3 us -> 51 us (0.975)
  Pallas kernels: 50.6 us -> 49.3 us
    pallas_call x1, Pallas kernels: 50.6 us -> 49.3 us  [per_device(): pl.pallas_call(kernel, out_shape=jax.ShapeDtypeStruct((2 * STEPS, WIDTH),...]
where the time goes in v2:
time: 51 us; the launch traced here: 50.8 us
  Pallas kernels  49.3 us (97%)
  local copies, waits for them, and re-layouts  1.47 us (3%)
    pallas_call x1, Pallas kernels, per_device(): pl.pallas_call(kernel, out_shape=jax.ShapeDtypeStruct((2 * STEPS, WIDTH),...  49.3 us
    unnamed x1, local copies, waits for them, and re-layouts  1.47 us

profile of v2, /device:TPU:6, one launch (start us, length us, event | category | flops | bytes accessed | tf_op | source)
XLA Modules:
  0.0 50.8 jit_solution(15170155566116371043)
XLA Ops:
  0.0 49.3 %shard_map.73 = f32[64,256]{1,0:T(8,128)} custom-call(f32[2,32,256]{2,1,0:T(8,128)} %guess_in.1, bf16[2,32,256]{2,1,0:T(8,128)(2,1)} %inputs_in.1, f32[2,256]{1,0:T(2,128)} %initial_in.1, f32[256,256]{1,0:T(8,128)} %base_in.1, bf16[256,256]{1,0:T(8,128)(2,1)} %weight_in.1, f32[1,256]{1,0:T(1,128)} %bitcast.4, f32[1,256]{1,0:T(1,128)} %bitcast.5), custom_call_target="tpu_custom_call" | custom-call | tf_op jit(solution)/shard_map/pallas_call | solution.py:525
  49.3 1.5 %copy.9 = f32[2,32,256]{2,1,0:T(8,128)} copy(f32[2,32,256]{2,1,0:T(8,128)} %bitcast.3) | data formatting | bytes 131072

commit v3 on v2

--- a/solution.py
+++ b/solution.py
@@ -17,6 +17,7 @@
 SUBS = STEPS // SUB
 ROWS = WIDTH + 16
 ZROOT = 1
+HALF = ROWS // 2
 
 
 def split(value):
@@ -60,8 +61,8 @@
     skew, skew_hi, skew_lo, diag, before, prev, pre, slope, offset, slope2, offset2, out2,
     part, start, first, second, third, own,
     ymaps, ywhole, zmaps, zwhole, half, whole,
-    pmaps, xin, cin, ein, xout, cout, zout, fin, entries, state,
-    isem, psem, ysend, yrecv, zsend, zrecv, hsem, csem, xsend, xrecv, esend, erecv, fsend, frecv,
+    pmaps, xin, cin, ein, xout, cout, zout, fin, entries, state, yheld, zheld,
+    isem, psem, ysend, yrecv, yrelay, zsend, zrecv, zrelay, hsem, csem, xsend, xrecv, esend, erecv, fsend, frecv,
 ):
     seq_at, grp_at = lax.axis_index("seq"), lax.axis_index("grp")
     x, c = seq_at // 2, seq_at % 2
@@ -74,16 +75,17 @@
     def block(index):
         return (index // 16, index % 16)
 
-    mine = y // 2
+    mine = 1 - y // 2
     yroot = c == y % 2
     zroot = yroot & (z == ZROOT)
     below = yroot & (z != ZROOT)
+    first_z, last_z = yroot & (z == 0), yroot & (z == 3)
     zroot0 = zroot & (c == 0)
     zroot1 = zroot & (c == 1)
-    root_at = [2 * s + c for s in range(2)]
+    root_at = [2 * (1 - s) + c for s in range(2)]
 
     def zroot_id(x, c):
-        return device(x, c, ZROOT, 2 * mine + c)
+        return device(x, c, ZROOT, 2 * (1 - mine) + c)
 
     fetches = [
         pltpu.make_async_copy(source, target, isem.at[index])
@@ -127,6 +129,10 @@
         for k in range(4):
             if k != ZROOT:
                 greet(device(x, c, k, y))
+
+    @pl.when(first_z)
+    def _():
+        greet(device(x, c, 3, y))
 
     for s in range(2):
 
@@ -220,6 +226,36 @@
             device_id_type=MESH,
         )
 
+    def to_far_root(s):
+        return pltpu.make_async_remote_copy(
+            src_ref=own.at[s, :HALF],
+            dst_ref=ymaps.at[y, :HALF],
+            send_sem=ysend.at[0],
+            recv_sem=yrecv.at[y],
+            device_id=device(x, c, z, (y + 2) % 4),
+            device_id_type=MESH,
+        )
+
+    def to_relay(s):
+        return pltpu.make_async_remote_copy(
+            src_ref=own.at[s, HALF:],
+            dst_ref=yheld,
+            send_sem=ysend.at[1],
+            recv_sem=yrelay.at[0],
+            device_id=device(x, c, z, (y + 3 - 2 * c) % 4),
+            device_id_type=MESH,
+        )
+
+    origin = (y + 1 + 2 * c) % 4
+    relayed = pltpu.make_async_remote_copy(
+        src_ref=yheld,
+        dst_ref=ymaps.at[origin, HALF:],
+        send_sem=yrelay.at[1],
+        recv_sem=yrecv.at[origin],
+        device_id=device(x, c, z, (origin + 2) % 4),
+        device_id_type=MESH,
+    )
+
     def landed(buffer, sem):
         return pltpu.make_async_remote_copy(
             src_ref=buffer,
@@ -230,12 +266,12 @@
             device_id_type=MESH,
         )
 
-    chains(0, 0, SUB)
+    chains(0, 0, SUB // 2)
 
     one, none = jnp.int32(1), jnp.int32(0)
     sends = jnp.where(place < 127, one, none) + jnp.where(yroot, 4 * one, 2 * one)
     sends = sends + jnp.where(below, one, none) + jnp.where(zroot, 15 * one, none)
-    sends = sends + jnp.where(zroot0, one, none) + jnp.where(zroot1 & (x < 3), 2 * one, none)
+    sends = sends + jnp.where(last_z, one, none) + jnp.where(zroot0, one, none) + jnp.where(zroot1 & (x < 3), 2 * one, none)
     pl.semaphore_wait(barrier, sends)
 
 
@@ -243,6 +279,7 @@
     def _():
         tail.start()
 
+    chains(0, SUB // 2, SUB)
     chains(1, 0, SUB // 2)
 
     @pl.when(place > 0)
@@ -272,18 +309,47 @@
         compose(second.at[s], first.at[s], part.at[s, 1])
         compose(own.at[s], second.at[s], third)
 
-        @pl.when(root_at[s] != y)
+        @pl.when(jnp.logical_not(yroot))
         def _():
             to_root(s).start()
 
-    to_zroot = pltpu.make_async_remote_copy(
-        src_ref=ywhole.at[3],
-        dst_ref=zmaps.at[z],
-        send_sem=zsend,
-        recv_sem=zrecv.at[z],
+        @pl.when(yroot & (mine != s))
+        def _():
+            to_relay(s).start()
+            to_far_root(s).start()
+
+    @pl.when(jnp.logical_not(yroot))
+    def _():
+        landed(yheld, yrelay.at[0]).wait_recv()
+        relayed.start()
+
+    def to_zroot(rows):
+        return pltpu.make_async_remote_copy(
+            src_ref=ywhole.at[3, rows],
+            dst_ref=zmaps.at[z, rows],
+            send_sem=zsend.at[0],
+            recv_sem=zrecv.at[z],
+            device_id=device(x, c, ZROOT, y),
+            device_id_type=MESH,
+        )
+
+    to_first_z = pltpu.make_async_remote_copy(
+        src_ref=ywhole.at[3, HALF:],
+        dst_ref=zheld,
+        send_sem=zsend.at[1],
+        recv_sem=zrelay.at[0],
+        device_id=device(x, c, 0, y),
+        device_id_type=MESH,
+    )
+    zrelayed = pltpu.make_async_remote_copy(
+        src_ref=zheld,
+        dst_ref=zmaps.at[3, HALF:],
+        send_sem=zrelay.at[1],
+        recv_sem=zrecv.at[3],
         device_id=device(x, c, ZROOT, y),
         device_id_type=MESH,
     )
+    near_z = below & (z != 3)
 
     @pl.when(yroot)
     def _():
@@ -297,9 +363,14 @@
             if k > 0:
                 compose(ywhole.at[k], ymaps.at[0] if k == 1 else ywhole.at[k - 1], ymaps.at[k])
 
-    @pl.when(below)
-    def _():
-        to_zroot.start()
+    @pl.when(near_z)
+    def _():
+        to_zroot(slice(0, ROWS)).start()
+
+    @pl.when(last_z)
+    def _():
+        to_first_z.start()
+        to_zroot(slice(0, HALF)).start()
 
     def prefix_out(k):
         return pltpu.make_async_remote_copy(
@@ -318,6 +389,11 @@
             @pl.when(y != k)
             def _():
                 prefix_out(k).start()
+
+    @pl.when(first_z)
+    def _():
+        landed(zheld, zrelay.at[0]).wait_recv()
+        zrelayed.start()
 
     across = pltpu.make_async_remote_copy(
         src_ref=zwhole.at[3],
@@ -471,15 +547,29 @@
     def _():
         tail.wait_send()
 
-    for s in range(2):
-
-        @pl.when(root_at[s] != y)
-        def _():
+    @pl.when(jnp.logical_not(yroot))
+    def _():
+        for s in range(2):
             to_root(s).wait_send()
-
-    @pl.when(below)
-    def _():
-        to_zroot.wait_send()
+        relayed.wait_send()
+
+    @pl.when(yroot)
+    def _():
+        to_relay(0).wait_send()
+        to_far_root(0).wait_send()
+
+    @pl.when(near_z)
+    def _():
+        to_zroot(slice(0, ROWS)).wait_send()
+
+    @pl.when(last_z)
+    def _():
+        to_first_z.wait_send()
+        to_zroot(slice(0, HALF)).wait_send()
+
+    @pl.when(first_z)
+    def _():
+        zrelayed.wait_send()
 
     @pl.when(zroot0 & (x == 0))
     def _():
@@ -569,12 +659,16 @@
             f32(2, 8, WIDTH),
             f32(2, 8, WIDTH),
             f32(8, WIDTH),
+            f32(HALF, WIDTH),
+            f32(HALF, WIDTH),
             dma((7,)),
             dma((2,)),
             dma((2,)),
             dma((4,)),
-            dma,
+            dma((2,)),
+            dma((2,)),
             dma((4,)),
+            dma((2,)),
             dma((2,)),
             dma((2,)),
             dma((2,)),

time: 51 us -> 51.2 us (level)
  no operation moved by 1% of the time
where the time goes in v3:
time: 51.2 us; the launch traced here: 51 us
  Pallas kernels  49.5 us (97%)
  local copies, waits for them, and re-layouts  1.47 us (3%)
    pallas_call x1, Pallas kernels, per_device(): pl.pallas_call(kernel, out_shape=jax.ShapeDtypeStruct((2 * STEPS, WIDTH),...  49.5 us
    unnamed x1, local copies, waits for them, and re-layouts  1.47 us

profile of v3, /device:TPU:6, one launch (start us, length us, event | category | flops | bytes accessed | tf_op | source)
XLA Modules:
  0.0 51.0 jit_solution(8854003687416685532)
XLA Ops:
  0.0 49.5 %shard_map.73 = f32[64,256]{1,0:T(8,128)} custom-call(f32[2,32,256]{2,1,0:T(8,128)} %guess_in.1, bf16[2,32,256]{2,1,0:T(8,128)(2,1)} %inputs_in.1, f32[2,256]{1,0:T(2,128)} %initial_in.1, f32[256,256]{1,0:T(8,128)} %base_in.1, bf16[256,256]{1,0:T(8,128)(2,1)} %weight_in.1, f32[1,256]{1,0:T(1,128)} %bitcast.4, f32[1,256]{1,0:T(1,128)} %bitcast.5), custom_call_target="tpu_custom_call" | custom-call | tf_op jit(solution)/shard_map/pallas_call | solution.py:615
  49.5 1.5 %copy.9 = f32[2,32,256]{2,1,0:T(8,128)} copy(f32[2,32,256]{2,1,0:T(8,128)} %bitcast.3) | data formatting | bytes 131072

commit v4 on v2

--- a/solution.py
+++ b/solution.py
@@ -16,7 +16,7 @@
 SUB = 8
 SUBS = STEPS // SUB
 ROWS = WIDTH + 16
-ZROOT = 1
+ZROOT = 3
 
 
 def split(value):
@@ -230,18 +230,28 @@
             device_id_type=MESH,
         )
 
-    chains(0, 0, SUB)
-
     one, none = jnp.int32(1), jnp.int32(0)
     sends = jnp.where(place < 127, one, none) + jnp.where(yroot, 4 * one, 2 * one)
     sends = sends + jnp.where(below, one, none) + jnp.where(zroot, 15 * one, none)
     sends = sends + jnp.where(zroot0, one, none) + jnp.where(zroot1 & (x < 3), 2 * one, none)
-    pl.semaphore_wait(barrier, sends)
-
-
-    @pl.when(place < 127)
-    def _():
-        tail.start()
+    late = (z == 3) & (y == 3)
+
+    def greeted():
+        pl.semaphore_wait(barrier, sends)
+
+        @pl.when(place < 127)
+        def _():
+            tail.start()
+
+    @pl.when(late)
+    def _():
+        greeted()
+
+    chains(0, 0, SUB)
+
+    @pl.when(jnp.logical_not(late))
+    def _():
+        greeted()
 
     chains(1, 0, SUB // 2)
 
@@ -288,14 +298,16 @@
     @pl.when(yroot)
     def _():
         ymaps[y] = own[mine]
-        for k in range(4):
+        for k in (2, 3, 0, 1):
 
             @pl.when(y != k)
             def _():
                 landed(ymaps.at[k], yrecv.at[k]).wait_recv()
 
-            if k > 0:
-                compose(ywhole.at[k], ymaps.at[0] if k == 1 else ywhole.at[k - 1], ymaps.at[k])
+            if k == 3:
+                compose(ywhole.at[0], ymaps.at[2], ymaps.at[3])
+        compose(ywhole.at[1], ymaps.at[0], ymaps.at[1])
+        compose(ywhole.at[3], ywhole.at[1], ywhole.at[0])
 
     @pl.when(below)
     def _():
@@ -313,6 +325,7 @@
 
     @pl.when(yroot)
     def _():
+        compose(ywhole.at[2], ywhole.at[1], ymaps.at[2])
         for k in range(1, 4):
 
             @pl.when(y != k)
@@ -361,11 +374,12 @@
 
     @pl.when(zroot)
     def _():
-        for k in range(4):
-            if k != ZROOT:
-                landed(zmaps.at[k], zrecv.at[k]).wait_recv()
-            if k > 0:
-                compose(zwhole.at[k], zprefix(k - 1), ywhole.at[3] if k == ZROOT else zmaps.at[k])
+        for k in (2, 0, 1):
+            landed(zmaps.at[k], zrecv.at[k]).wait_recv()
+            if k == 2:
+                compose(zwhole.at[0], zmaps.at[2], ywhole.at[3])
+        compose(zwhole.at[1], zmaps.at[0], zmaps.at[1])
+        compose(zwhole.at[3], zwhole.at[1], zwhole.at[0])
 
         @pl.when((c == 0) & (x == 0))
         def _():
@@ -373,15 +387,18 @@
             ein[...] = tile(given)
             cout[...] = tile(applied(as_columns(given), zwhole.at[3]))
             across0.start()
+            compose(zwhole.at[2], zwhole.at[1], zmaps.at[2])
 
         @pl.when((c == 0) & (x > 0))
         def _():
             across.start()
+            compose(zwhole.at[2], zwhole.at[1], zmaps.at[2])
             landed(xin, xrecv).wait_recv()
             ein[...] = xin[...]
 
         @pl.when((c == 1) & (x == 0))
         def _():
+            compose(zwhole.at[2], zwhole.at[1], zmaps.at[2])
             across0.wait_recv()
             ein[...] = cin[...]
             xout[...] = tile(applied(as_columns(cin[0:1, :]), zwhole.at[3]))
@@ -390,6 +407,7 @@
 
         @pl.when((c == 1) & (x > 0))
         def _():
+            compose(zwhole.at[2], zwhole.at[1], zmaps.at[2])
             across.wait_recv()
             compose(whole, half, zwhole.at[3])
             landed(xin, xrecv).wait_recv()

time: 51 us -> 49.2 us (0.965)
  Pallas kernels: 49.3 us -> 47.5 us
    pallas_call x1, Pallas kernels: 49.3 us -> 47.5 us  [per_device(): pl.pallas_call(kernel, out_shape=jax.ShapeDtypeStruct((2 * STEPS, WIDTH),...]
where the time goes in v4:
time: 49.2 us; the launch traced here: 49 us
  Pallas kernels  47.5 us (97%)
  local copies, waits for them, and re-layouts  1.47 us (3%)
    pallas_call x1, Pallas kernels, per_device(): pl.pallas_call(kernel, out_shape=jax.ShapeDtypeStruct((2 * STEPS, WIDTH),...  47.5 us
    unnamed x1, local copies, waits for them, and re-layouts  1.47 us

profile of v4, /device:TPU:6, one launch (start us, length us, event | category | flops | bytes accessed | tf_op | source)
XLA Modules:
  0.0 49.0 jit_solution(12224536635981067184)
XLA Ops:
  0.0 47.5 %shard_map.73 = f32[64,256]{1,0:T(8,128)} custom-call(f32[2,32,256]{2,1,0:T(8,128)} %guess_in.1, bf16[2,32,256]{2,1,0:T(8,128)(2,1)} %inputs_in.1, f32[2,256]{1,0:T(2,128)} %initial_in.1, f32[256,256]{1,0:T(8,128)} %base_in.1, bf16[256,256]{1,0:T(8,128)(2,1)} %weight_in.1, f32[1,256]{1,0:T(1,128)} %bitcast.4, f32[1,256]{1,0:T(1,128)} %bitcast.5), custom_call_target="tpu_custom_call" | custom-call | tf_op jit(solution)/shard_map/pallas_call | solution.py:543
  47.5 1.5 %copy.9 = f32[2,32,256]{2,1,0:T(8,128)} copy(f32[2,32,256]{2,1,0:T(8,128)} %bitcast.3) | data formatting | bytes 131072

commit v5 on v4

--- a/solution.py
+++ b/solution.py
@@ -15,7 +15,7 @@
 STEPS = 32
 SUB = 8
 SUBS = STEPS // SUB
-ROWS = WIDTH + 16
+ROWS = WIDTH + 8
 ZROOT = 3
 
 
@@ -46,7 +46,11 @@
 
 
 def applied(columns, whole):
-    moved = jnp.sum(whole[:WIDTH, :] * columns, axis=0, keepdims=True)
+    parts = [
+        jnp.sum(whole[at : at + 64, :] * columns[at : at + 64, :], axis=0, keepdims=True)
+        for at in range(0, WIDTH, 64)
+    ]
+    moved = (parts[0] + parts[1]) + (parts[2] + parts[3])
     return moved + whole[WIDTH : WIDTH + 1, :]
 
 
@@ -153,7 +157,7 @@
     square = (WIDTH, WIDTH)
     eye = lax.broadcasted_iota(jnp.int32, square, 0) == lax.broadcasted_iota(jnp.int32, square, 1)
     diag[...] = jnp.where(eye, jnp.broadcast_to(keep, square), 0.0)
-    top = (lax.broadcasted_iota(jnp.int32, (16, WIDTH), 0) == 0).astype(F32)
+    top = (lax.broadcasted_iota(jnp.int32, (8, WIDTH), 0) == 0).astype(F32)
 
     fetches[0].wait()
     for s in range(2):
@@ -184,22 +188,23 @@
         target[:WIDTH, :] = diag[...] + skew[...] * slope[at : at + 1, :]
         target[WIDTH:, :] = top * offset[at : at + 1, :]
 
-    def chains(s, begin, end):
+    def chains(begin, end):
         for inner in range(begin, end):
-            if inner == 0:
+            for s in range(2):
                 for sub in range(SUBS):
-                    of_step(part.at[s, sub], s * STEPS + max(sub * SUB, 1))
-                continue
-            for sub in range(SUBS):
-                at = max(sub * SUB, 1) + inner
-                if at == SUB * (sub + 1):
-                    continue
-                at = at + s * STEPS
-                held = part[s, sub]
-                turned = dot3(held, skew_hi[...], skew_lo[...])
-                moved = keep * held + slope[at : at + 1, :] * turned
-                part[s, sub, :WIDTH, :] = moved[:WIDTH]
-                part[s, sub, WIDTH:, :] = moved[WIDTH:] + top * offset[at : at + 1, :]
+                    first_at = max(sub * SUB, 1)
+                    at = first_at + inner
+                    if at == SUB * (sub + 1):
+                        continue
+                    at = at + s * STEPS
+                    if inner == 0:
+                        of_step(part.at[s, sub], at)
+                        continue
+                    held = part[s, sub]
+                    turned = dot3(held, skew_hi[...], skew_lo[...])
+                    moved = keep * held + slope[at : at + 1, :] * turned
+                    part[s, sub, :WIDTH, :] = moved[:WIDTH]
+                    part[s, sub, WIDTH:, :] = moved[WIDTH:] + top * offset[at : at + 1, :]
 
     tail = pltpu.make_async_remote_copy(
         src_ref=guess.at[:, STEPS - 8 :, :],
@@ -247,13 +252,13 @@
     def _():
         greeted()
 
-    chains(0, 0, SUB)
+    chains(0, SUB // 2)
 
     @pl.when(jnp.logical_not(late))
     def _():
         greeted()
 
-    chains(1, 0, SUB // 2)
+    chains(SUB // 2, SUB)
 
     @pl.when(place > 0)
     def _():
@@ -274,13 +279,14 @@
         keep_slopes(slice(t * STEPS, t * STEPS + 8), steep[rows], added[rows])
 
     for s in range(2):
-        if s == 1:
-            chains(1, SUB // 2, SUB)
-        of_step(start, s * STEPS)
-        compose(third, part.at[s, 2], part.at[s, 3])
-        compose(first.at[s], start, part.at[s, 0])
+        of_step(start.at[s], s * STEPS)
+        compose(third.at[s], part.at[s, 2], part.at[s, 3])
+        compose(first.at[s], start.at[s], part.at[s, 0])
+    for s in range(2):
         compose(second.at[s], first.at[s], part.at[s, 1])
-        compose(own.at[s], second.at[s], third)
+    for s in range(2):
+        compose(own.at[s], second.at[s], third.at[s])
+    for s in range(2):
 
         @pl.when(root_at[s] != y)
         def _():
@@ -402,24 +408,34 @@
             across0.wait_recv()
             ein[...] = cin[...]
             xout[...] = tile(applied(as_columns(cin[0:1, :]), zwhole.at[3]))
-            for core in (1, 0):
+            for core in (0, 1):
                 onward(core).start()
 
         @pl.when((c == 1) & (x > 0))
         def _():
             compose(zwhole.at[2], zwhole.at[1], zmaps.at[2])
             across.wait_recv()
-            compose(whole, half, zwhole.at[3])
+
+            @pl.when(x == 2)
+            def _():
+                compose(whole, half, zwhole.at[3])
+
             landed(xin, xrecv).wait_recv()
             columns = as_columns(xin[0:1, :])
 
-            @pl.when(x < 3)
+            @pl.when(x == 2)
             def _():
                 xout[...] = tile(applied(columns, whole))
-                for core in (1, 0):
+                for core in (0, 1):
                     onward(core).start()
 
             ein[...] = tile(applied(columns, half))
+
+            @pl.when(x == 1)
+            def _():
+                xout[...] = tile(applied(as_columns(ein[0:1, :]), zwhole.at[3]))
+                for core in (0, 1):
+                    onward(core).start()
 
         columns = as_columns(ein[0:1, :])
         for k in range(4):
@@ -509,7 +525,7 @@
 
     @pl.when(zroot1 & (x < 3))
     def _():
-        for core in (1, 0):
+        for core in (0, 1):
             onward(core).wait_send()
 
     @pl.when(zroot)
@@ -566,10 +582,10 @@
             f32(2, 2 * STEPS, 128),
             f32(2, 2 * STEPS, 128),
             f32(2, SUBS, *maps),
-            f32(*maps),
             f32(2, *maps),
             f32(2, *maps),
-            f32(*maps),
+            f32(2, *maps),
+            f32(2, *maps),
             f32(2, *maps),
             f32(4, *maps),
             f32(4, *maps),

time: 49.2 us -> 47.6 us (0.967)
  Pallas kernels: 47.5 us -> 46 us
    pallas_call x1, Pallas kernels: 47.5 us -> 46 us  [per_device(): pl.pallas_call(kernel, out_shape=jax.ShapeDtypeStruct((2 * STEPS, WIDTH),...]
where the time goes in v5:
time: 47.6 us; the launch traced here: 47.5 us
  Pallas kernels  46 us (97%)
  local copies, waits for them, and re-layouts  1.47 us (3%)
    pallas_call x1, Pallas kernels, per_device(): pl.pallas_call(kernel, out_shape=jax.ShapeDtypeStruct((2 * STEPS, WIDTH),...  46 us
    unnamed x1, local copies, waits for them, and re-layouts  1.47 us

profile of v5, /device:TPU:6, one launch (start us, length us, event | category | flops | bytes accessed | tf_op | source)
XLA Modules:
  0.0 47.5 jit_solution(2313695371443878760)
XLA Ops:
  0.0 46.0 %shard_map.73 = f32[64,256]{1,0:T(8,128)} custom-call(f32[2,32,256]{2,1,0:T(8,128)} %guess_in.1, bf16[2,32,256]{2,1,0:T(8,128)(2,1)} %inputs_in.1, f32[2,256]{1,0:T(2,128)} %initial_in.1, f32[256,256]{1,0:T(8,128)} %base_in.1, bf16[256,256]{1,0:T(8,128)(2,1)} %weight_in.1, f32[1,256]{1,0:T(1,128)} %bitcast.4, f32[1,256]{1,0:T(1,128)} %bitcast.5), custom_call_target="tpu_custom_call" | custom-call | tf_op jit(solution)/shard_map/pallas_call | solution.py:559
  46.0 1.5 %copy.9 = f32[2,32,256]{2,1,0:T(8,128)} copy(f32[2,32,256]{2,1,0:T(8,128)} %bitcast.3) | data formatting | bytes 131072

commit v6 on v5

--- a/solution.py
+++ b/solution.py
@@ -142,9 +142,15 @@
     def _():
         greet(zroot_id(x, 0))
 
+    inner_slab = (x == 1) | (x == 2)
+
+    @pl.when(zroot0 & inner_slab)
+    def _():
+        greet(zroot_id(x, 1))
+
     @pl.when(zroot & (x > 0))
     def _():
-        greet(zroot_id(x - 1, 1))
+        greet(zroot_id(x - 1, jnp.where(x == 1, 1, c)))
 
     fetches[3].wait()
     skew_t = jnp.transpose(base[...]) - base[...]
@@ -238,7 +244,9 @@
     one, none = jnp.int32(1), jnp.int32(0)
     sends = jnp.where(place < 127, one, none) + jnp.where(yroot, 4 * one, 2 * one)
     sends = sends + jnp.where(below, one, none) + jnp.where(zroot, 15 * one, none)
-    sends = sends + jnp.where(zroot0, one, none) + jnp.where(zroot1 & (x < 3), 2 * one, none)
+    sends = sends + jnp.where(zroot0, one, none) + jnp.where(zroot1 & (x == 0), 2 * one, none)
+    sends = sends + jnp.where(zroot & inner_slab, one, none)
+    sends = sends + jnp.where(zroot1 & inner_slab, one, none)
     late = (z == 3) & (y == 3)
 
     def greeted():
@@ -344,6 +352,14 @@
         send_sem=hsem.at[0],
         recv_sem=hsem.at[1],
         device_id=zroot_id(x, 1),
+        device_id_type=MESH,
+    )
+    back = pltpu.make_async_remote_copy(
+        src_ref=zwhole.at[3],
+        dst_ref=half,
+        send_sem=hsem.at[0],
+        recv_sem=hsem.at[1],
+        device_id=zroot_id(x, 0),
         device_id_type=MESH,
     )
     across0 = pltpu.make_async_remote_copy(
@@ -399,8 +415,20 @@
         def _():
             across.start()
             compose(zwhole.at[2], zwhole.at[1], zmaps.at[2])
+
+            @pl.when(x < 3)
+            def _():
+                landed(half, hsem.at[1]).wait_recv()
+                compose(whole, zwhole.at[3], half)
+
             landed(xin, xrecv).wait_recv()
             ein[...] = xin[...]
+
+            @pl.when(x < 3)
+            def _():
+                xout[...] = tile(applied(as_columns(xin[0:1, :]), whole))
+                onward(0).start()
+
 
         @pl.when((c == 1) & (x == 0))
         def _():
@@ -413,6 +441,10 @@
 
         @pl.when((c == 1) & (x > 0))
         def _():
+            @pl.when(x < 3)
+            def _():
+                back.start()
+
             compose(zwhole.at[2], zwhole.at[1], zmaps.at[2])
             across.wait_recv()
 
@@ -426,16 +458,14 @@
             @pl.when(x == 2)
             def _():
                 xout[...] = tile(applied(columns, whole))
-                for core in (0, 1):
-                    onward(core).start()
+                onward(1).start()
 
             ein[...] = tile(applied(columns, half))
 
             @pl.when(x == 1)
             def _():
                 xout[...] = tile(applied(as_columns(ein[0:1, :]), zwhole.at[3]))
-                for core in (0, 1):
-                    onward(core).start()
+                onward(1).start()
 
         columns = as_columns(ein[0:1, :])
         for k in range(4):
@@ -523,10 +553,17 @@
     def _():
         across.wait_send()
 
+    @pl.when(zroot1 & inner_slab)
+    def _():
+        back.wait_send()
+
     @pl.when(zroot1 & (x < 3))
     def _():
-        for core in (0, 1):
-            onward(core).wait_send()
+        onward(1).wait_send()
+
+    @pl.when((zroot1 & (x == 0)) | (zroot0 & inner_slab))
+    def _():
+        onward(0).wait_send()
 
     @pl.when(zroot)
     def _():

time: 47.6 us -> 47.4 us (level)
  no operation moved by 1% of the time
where the time goes in v6:
time: 47.4 us; the launch traced here: 47.3 us
  Pallas kernels  45.8 us (97%)
  local copies, waits for them, and re-layouts  1.47 us (3%)
    pallas_call x1, Pallas kernels, per_device(): pl.pallas_call(kernel, out_shape=jax.ShapeDtypeStruct((2 * STEPS, WIDTH),...  45.8 us
    unnamed x1, local copies, waits for them, and re-layouts  1.47 us

profile of v6, /device:TPU:6, one launch (start us, length us, event | category | flops | bytes accessed | tf_op | source)
XLA Modules:
  0.0 47.3 jit_solution(14224255512447624638)
XLA Ops:
  0.0 45.8 %shard_map.73 = f32[64,256]{1,0:T(8,128)} custom-call(f32[2,32,256]{2,1,0:T(8,128)} %guess_in.1, bf16[2,32,256]{2,1,0:T(8,128)(2,1)} %inputs_in.1, f32[2,256]{1,0:T(2,128)} %initial_in.1, f32[256,256]{1,0:T(8,128)} %base_in.1, bf16[256,256]{1,0:T(8,128)(2,1)} %weight_in.1, f32[1,256]{1,0:T(1,128)} %bitcast.4, f32[1,256]{1,0:T(1,128)} %bitcast.5), custom_call_target="tpu_custom_call" | custom-call | tf_op jit(solution)/shard_map/pallas_call | solution.py:596
  45.8 1.5 %copy.9 = f32[2,32,256]{2,1,0:T(8,128)} copy(f32[2,32,256]{2,1,0:T(8,128)} %bitcast.3) | data formatting | bytes 131072

commit v7 on v6

--- a/solution.py
+++ b/solution.py
@@ -503,12 +503,12 @@
         def _():
             landed(fin.at[s], erecv.at[s]).wait_recv()
 
-        given = fin[s, 0:1, :]
-        entries[s] = fin[s]
-
-        @pl.when(y > 0)
-        def _():
-            entries[s] = tile(applied(as_columns(given), pmaps.at[s]))
+    entries[...] = fin[...]
+
+    @pl.when(y > 0)
+    def _():
+        for s in range(2):
+            entries[s] = tile(applied(as_columns(fin[s, 0:1, :]), pmaps.at[s]))
 
     for s in range(2):
         entry = entries[s, 0:1, :]

time: 47.4 us -> 47.4 us (level)
  no operation moved by 1% of the time
where the time goes in v7:
time: 47.4 us; the launch traced here: 47.3 us
  Pallas kernels  45.8 us (97%)
  local copies, waits for them, and re-layouts  1.47 us (3%)
    pallas_call x1, Pallas kernels, per_device(): pl.pallas_call(kernel, out_shape=jax.ShapeDtypeStruct((2 * STEPS, WIDTH),...  45.8 us
    unnamed x1, local copies, waits for them, and re-layouts  1.47 us

profile of v7, /device:TPU:6, one launch (start us, length us, event | category | flops | bytes accessed | tf_op | source)
XLA Modules:
  0.0 47.3 jit_solution(11958008897089832825)
XLA Ops:
  0.0 45.8 %shard_map.73 = f32[64,256]{1,0:T(8,128)} custom-call(f32[2,32,256]{2,1,0:T(8,128)} %guess_in.1, bf16[2,32,256]{2,1,0:T(8,128)(2,1)} %inputs_in.1, f32[2,256]{1,0:T(2,128)} %initial_in.1, f32[256,256]{1,0:T(8,128)} %base_in.1, bf16[256,256]{1,0:T(8,128)(2,1)} %weight_in.1, f32[1,256]{1,0:T(1,128)} %bitcast.4, f32[1,256]{1,0:T(1,128)} %bitcast.5), custom_call_target="tpu_custom_call" | custom-call | tf_op jit(solution)/shard_map/pallas_call | solution.py:596
  45.8 1.5 %copy.9 = f32[2,32,256]{2,1,0:T(8,128)} copy(f32[2,32,256]{2,1,0:T(8,128)} %bitcast.3) | data formatting | bytes 131072
